TPU v7x, 512 devices: a whole 4x4x16 slice. The times are simulated.
512 devices in a mesh: segment: 32 (over z, core), neuron: 16 (over y, x).
Axes of the slice: x: 4, y: 4, z: 16, core: 2. Of those that a mesh axis runs over, the one named last changes fastest.
Arguments:
- pending_minibatch: bfloat16 [32, 8, 65536], P('segment', None, 'neuron'), may hold values from 0 to 32
- arriving_minibatches: bfloat16 [1, 8, 65536], P(None, None, 'neuron'), may hold values from 0 to 32
- coefficient_tiles: bfloat16 [32, 2, 4, 64, 65536], P('segment', None, None, None, 'neuron'), may hold values from -0.375 to 0.375
- offset_vector: float32 [32, 2, 65536], P('segment', None, 'neuron'), may hold values from -4 to 2
- source_tile_lookup: int32 [32, 2, 4, 1024], P('segment', None, None, 'neuron'), may hold values from 0 to 1023, as said below
- depth_of_segment: int32 [32], P('segment'), may hold values from 1 to 2, as said below
Outputs:
- section_out: bfloat16 [32, 8, 65536], P('segment', None, 'neuron')
Inputs may be any that keep to these rules, and one draw needn't show every extreme that they name: `depth_of_segment`: every section has at least one layer and some section has 2. `source_tile_lookup`: for each section, layer and group of 64 consecutive output blocks, the 256 entries name input blocks from each of the 16 groups of 64 consecutive input blocks exactly equally often.
All inputs are finite; a program needn't handle non-finite values.
Results may differ from a plain program's by a relative error of at most 0.0051.
Values may be sent and summed in bfloat16 or wider, within the bound.
A program may use at most 128 MiB of HBM per device.

v0:
```python
import jax
import jax.numpy as jnp
from jax import lax
from jax.sharding import PartitionSpec as P

BLK = 64
KB = 4
LMAX = 2


def shifted(value, axis, by):
    size = lax.axis_size(axis)
    pairs = [(i, i + by) for i in range(size) if 0 <= i + by < size]
    return lax.ppermute(value, axis, pairs)


def run_layer(y, w, b, idx):
    rows = y.shape[0]
    blocks_here = idx.shape[1]
    w_blocks = w.reshape(KB, BLK, blocks_here, BLK)
    cols = idx[:, :, None] * BLK + jnp.arange(BLK, dtype=jnp.int32)[None, None, :]
    full = lax.all_gather(y, "neuron", axis=1, tiled=True)
    taken = jnp.take(full, cols.reshape(-1), axis=1).reshape(rows, KB, blocks_here, BLK)
    acc = jnp.einsum("bkjr,krjc->bjc", taken, w_blocks, preferred_element_type=jnp.float32)
    acc = acc.reshape(rows, blocks_here * BLK)
    return jnp.clip(acc + b[None, :], 0.0, 32.0).astype(jnp.bfloat16)


def apply_layer_section(y, coefficient_tiles, offset_vector, source_tile_lookup, stored_tile_total):
    for level in range(LMAX):
        fresh = run_layer(
            y, coefficient_tiles[level], offset_vector[level], source_tile_lookup[level]
        )
        y = jnp.where(level < stored_tile_total, fresh, y)
    return y


def per_device(
    pending_minibatch,
    arriving_minibatches,
    coefficient_tiles,
    offset_vector,
    source_tile_lookup,
    depth_of_segment,
):
    coefficient_slice_local = coefficient_tiles[0]
    offset_slice_local = offset_vector[0]
    slice_tile_lookup = source_tile_lookup[0]
    stored_tile_total = depth_of_segment[0]
    activation_matrix = apply_layer_section(
        pending_minibatch[0],
        coefficient_slice_local,
        offset_slice_local,
        slice_tile_lookup,
        stored_tile_total,
    )
    first_phase = lax.axis_index("segment") == 0
    moved = shifted(activation_matrix, "segment", 1)
    moved = jnp.where(first_phase, arriving_minibatches[0], moved)
    activation_matrix = apply_layer_section(
        moved, coefficient_slice_local, offset_slice_local, slice_tile_lookup, stored_tile_total
    )
    return activation_matrix[None]


def solution(mesh):
    placed = (
        P("segment", None, "neuron"),
        P(None, None, "neuron"),
        P("segment", None, None, None, "neuron"),
        P("segment", None, "neuron"),
        P("segment", None, None, "neuron"),
        P("segment"),
    )
    return jax.shard_map(
        per_device,
        mesh=mesh,
        in_specs=placed,
        out_specs=P("segment", None, "neuron"),
        check_vma=False,
    )
```

profile of v0, /device:TPU:1, one launch (start us, length us, event | category | flops | bytes accessed | tf_op | source)
XLA Modules:
  0.0 870.1 jit_solution(10240029558922843930)
XLA Ops:
  6.5 0.0 all-gather.12.cloned.1.call-start
  6.5 2.3 copy.36
  8.8 0.0 all-gather.12.cloned.1.call-update
  8.8 0.0 all-gather.6.cloned.1.call-start
  8.9 0.7 multiply_bitcast_fusion
  9.6 4.1 fusion.34
  13.6 0.8 iota_add_fusion
  14.4 0.1 add.45
  14.5 6.9 reshape_squeeze.8
  22.1 0.0 copy-done.10
  22.1 120.2 %all-gather.12.cloned.1.call-done = bf16[1,8,65536]{1,2,0:T(8,128)(2,1)} async-done(((bf16[1,8,4096]{1,2,0:T(8,128)(2,1)}), bf16[1,8,65536]{1,2,0:T(8,128)(2,1)}) %all-gather.12.cloned.1.call-update) | async-done | bytes 1048592 | tf_op jit(solution)/shard_map/all_gather | solution.py:22
  142.3 62.8 %gather_fusion = bf16[16384,8]{1,0:T(8,128)(2,1)} fusion(bf16[8,65536]{0,1:T(8,128)(2,1)} %bitcast.87, s32[16384]{0:T(1024)S(1)} %fusion.32), kind=kCustom, calls=%fused_computation.clone | custom fusion | bytes 589824 | tf_op jit(solution)/shard_map/jit(_take)/gather | solution.py:23
  205.1 11.1 %broadcast_select_fusion.2 = bf16[16384,8]{1,0:T(8,128)(2,1)S(1)} fusion(bf16[16384,8]{1,0:T(8,128)(2,1)} %gather_fusion, pred[16384]{0:T(1024)(128)(4,1)S(1)} %compare_and_fusion.1), kind=kLoop, calls=%fused_computation.6 | loop fusion | flops 131072 | bytes 540672 | tf_op jit(solution)/shard_map/jit(_take)/select_n | solution.py:23
  216.2 4.6 fusion.16
  220.8 2.0 copy.61
  222.8 2.8 fusion.28
  225.6 0.0 all-gather.6.cloned.1.call-update
  225.6 0.5 all-gather.8.cloned.1.call-start
  226.1 0.1 add.96
  226.2 5.6 reshape_squeeze.9
  231.9 120.3 %all-gather.6.cloned.1.call-done = bf16[8,65536]{0,1:T(8,128)(2,1)} async-done(((bf16[8,4096]{0,1:T(8,128)(2,1)}), bf16[8,65536]{0,1:T(8,128)(2,1)}) %all-gather.6.cloned.1.call-update) | async-done | bytes 1048592 | tf_op jit(solution)/shard_map/all_gather | solution.py:22
  352.2 62.8 %gather_fusion.1 = bf16[16384,8]{1,0:T(8,128)(2,1)} fusion(bf16[8,65536]{0,1:T(8,128)(2,1)} %all-gather.6.cloned.1.call-done, s32[16384]{0:T(1024)S(1)} %fusion.33), kind=kCustom, calls=%fused_computation.1.clone | custom fusion | bytes 589824 | tf_op jit(solution)/shard_map/jit(_take)/gather | solution.py:23
  415.0 11.1 %broadcast_select_fusion = bf16[16384,8]{1,0:T(8,128)(2,1)S(1)} fusion(bf16[16384,8]{1,0:T(8,128)(2,1)} %gather_fusion.1, pred[16384]{0:T(1024)(128)(4,1)S(1)} %compare_and_fusion), kind=kLoop, calls=%fused_computation.4 | loop fusion | flops 131072 | bytes 540672 | tf_op jit(solution)/shard_map/jit(_take)/select_n | solution.py:23
  426.1 4.6 fusion.22
  430.7 2.0 copy.62
  432.7 1.9 fusion.29
  434.6 0.3 copy.46
  434.9 3.8 collective-permute-start
  438.7 0.5 copy.35
  439.2 0.8 collective-permute-done
  440.0 0.5 copy.47
  440.5 1.1 bitcast_select_fusion
  441.6 0.0 all-gather.8.cloned.1.call-update
  441.7 0.2 all-gather.10.cloned.1.call-start
  441.9 128.1 %all-gather.8.cloned.1.call-done = bf16[8,65536]{0,1:T(8,128)(2,1)} async-done(((bf16[8,4096]{0,1:T(8,128)(2,1)}), bf16[8,65536]{0,1:T(8,128)(2,1)}) %all-gather.8.cloned.1.call-update) | async-done | bytes 1048592 | tf_op jit(solution)/shard_map/all_gather | solution.py:22
  569.9 62.8 %gather_fusion.2 = bf16[16384,8]{1,0:T(8,128)(2,1)} fusion(bf16[8,65536]{0,1:T(8,128)(2,1)} %all-gather.8.cloned.1.call-done, s32[16384]{0:T(1024)S(1)} %fusion.32), kind=kCustom, calls=%fused_computation.2.clone | custom fusion | bytes 589824 | tf_op jit(solution)/shard_map/jit(_take)/gather | solution.py:23
  632.8 11.1 %broadcast_select_fusion.3 = bf16[16384,8]{1,0:T(8,128)(2,1)S(1)} fusion(bf16[16384,8]{1,0:T(8,128)(2,1)} %gather_fusion.2, pred[16384]{0:T(1024)(128)(4,1)S(1)} %compare_and_fusion.1), kind=kLoop, calls=%fused_computation.7 | loop fusion | flops 131072 | bytes 540672 | tf_op jit(solution)/shard_map/jit(_take)/select_n | solution.py:23
  643.9 4.6 fusion.19
  648.5 2.0 copy.63
  650.4 2.7 fusion.30
  653.1 0.0 all-gather.10.cloned.1.call-update
  653.2 126.6 %all-gather.10.cloned.1.call-done = bf16[8,65536]{0,1:T(8,128)(2,1)} async-done(((bf16[8,4096]{0,1:T(8,128)(2,1)}), bf16[8,65536]{0,1:T(8,128)(2,1)}) %all-gather.10.cloned.1.call-update) | async-done | bytes 1048592 | tf_op jit(solution)/shard_map/all_gather | solution.py:22
  779.8 62.8 %gather_fusion.3 = bf16[16384,8]{1,0:T(8,128)(2,1)} fusion(bf16[8,65536]{0,1:T(8,128)(2,1)} %all-gather.10.cloned.1.call-done, s32[16384]{0:T(1024)S(1)} %fusion.33), kind=kCustom, calls=%fused_computation.3.clone | custom fusion | bytes 589824 | tf_op jit(solution)/shard_map/jit(_take)/gather | solution.py:23
  842.5 11.3 %broadcast_select_fusion.1 = bf16[16384,8]{1,0:T(8,128)(2,1)S(1)} fusion(bf16[16384,8]{1,0:T(8,128)(2,1)} %gather_fusion.3, pred[16384]{0:T(1024)(128)(4,1)S(1)} %compare_and_fusion), kind=kLoop, calls=%fused_computation.5 | loop fusion | flops 131072 | bytes 540672 | tf_op jit(solution)/shard_map/jit(_take)/select_n | solution.py:23
  853.9 4.6 fusion.25
  858.4 2.0 copy.64
  860.4 1.9 fusion.31
  862.4 0.9 copy.56
  (26 shorter events, 0.2 us)
Async XLA Ops:
  6.5 135.8 %all-gather.12.cloned.1.call-start = ((), (), s32[]{:S(2)}) async-start(), calls=%async_computation.3 | async-start | bytes 17825792 | tf_op jit(solution)/shard_map/all_gather | solution.py:22
  8.8 343.4 %all-gather.6.cloned.1.call-start = ((), (), s32[]{:S(2)}) async-start(), calls=%async_computation | async-start | bytes 17825792 | tf_op jit(solution)/shard_map/all_gather | solution.py:22
  13.6 8.5 copy-start.10
  205.1 11.1 %copy-start = (bf16[4,64,64,64]{3,2,1,0:T(8,128)(2,1)S(1)}, bf16[4,64,64,64]{3,2,1,0:T(8,128)(2,1)}, u32[]{:S(2)}) copy-start(bf16[4,64,64,64]{3,2,1,0:T(8,128)(2,1)} %reshape_squeeze.8) | copy-start | bytes 6291460
  216.2 6.6 copy-start.6
  222.8 3.3 copy-start.8
  225.6 344.4 %all-gather.8.cloned.1.call-start = ((), (), s32[]{:S(2)}) async-start(), calls=%async_computation.1 | async-start | bytes 17825792 | tf_op jit(solution)/shard_map/all_gather | solution.py:22
  415.0 11.1 %copy-start.2 = (bf16[4,64,64,64]{3,2,1,0:T(8,128)(2,1)S(1)}, bf16[4,64,64,64]{3,2,1,0:T(8,128)(2,1)}, u32[]{:S(2)}) copy-start(bf16[4,64,64,64]{3,2,1,0:T(8,128)(2,1)} %reshape_squeeze.9) | copy-start | bytes 6291460
  426.1 6.6 copy-start.4
  430.7 8.0 copy-start.9
  434.9 5.1 collective-permute-start
  441.7 338.1 %all-gather.10.cloned.1.call-start = ((), (), s32[]{:S(2)}) async-start(), calls=%async_computation.2 | async-start | bytes 17825792 | tf_op jit(solution)/shard_map/all_gather | solution.py:22
  632.8 11.1 %copy-start.1 = (bf16[4,64,64,64]{3,2,1,0:T(8,128)(2,1)S(1)}, bf16[4,64,64,64]{3,2,1,0:T(8,128)(2,1)}, u32[]{:S(2)}) copy-start(bf16[4,64,64,64]{3,2,1,0:T(8,128)(2,1)} %reshape_squeeze.8) | copy-start | bytes 6291460
  643.9 6.6 copy-start.7
  842.5 11.3 %copy-start.3 = (bf16[4,64,64,64]{3,2,1,0:T(8,128)(2,1)S(1)}, bf16[4,64,64,64]{3,2,1,0:T(8,128)(2,1)}, u32[]{:S(2)}) copy-start(bf16[4,64,64,64]{3,2,1,0:T(8,128)(2,1)} %reshape_squeeze.9) | copy-start | bytes 6291460
  853.8 6.6 copy-start.5
Sparse Core Ops, SparseCore 0:
  10.4 131.8 all-gather.11
  225.7 126.4 all-gather.5
  441.8 128.1 all-gather.7
  653.3 126.4 all-gather.9
where the time goes:
time: 879 us; the launch traced here: 870 us
  waiting for transfers between devices  496 us (56%)
  local copies, waits for them, and re-layouts  280 us (32%)
  other arithmetic  56.6 us (6%)
  matrix products  18.3 us (2%)
  between operations  14.2 us (2%)
    all_gather x4, waiting for transfers between devices, run_layer(): full = lax.all_gather(y, 'neuron', axis=1, tiled=True)  495 us
    gather x4, local copies, waits for them, and re-layouts, run_layer(): jnp.take(full, cols.reshape(-1), axis=1).reshape(rows, KB, blocks_here, BLK)  251 us
    select_n x4, other arithmetic, run_layer(): jnp.take(full, cols.reshape(-1), axis=1).reshape(rows, KB, blocks_here, BLK)  44.5 us
    dot_general x4, matrix products, run_layer(): jnp.einsum('bkjr,krjc->bjc', taken, w_blocks, preferred_element_type=jnp....  18.3 us
  transfers between devices with their start and end apart: 5, of which 5 were waited for; matrix products, arithmetic and copies ran while one was open for 2% of the time, Pallas kernels for 0%

commit v1 on v0

--- a/solution.py
+++ b/solution.py
@@ -6,6 +6,24 @@
 BLK = 64
 KB = 4
 LMAX = 2
+
+
+def collect(array, axis, dim):
+    ways, here, step = (lax.axis_size(axis), lax.axis_index(axis), array.shape[dim])
+    shape = [n * ways if d == dim else n for d, n in enumerate(array.shape)]
+    full = lax.dynamic_update_slice_in_dim(
+        jnp.zeros(shape, array.dtype), array, here * step, axis=dim
+    )
+    going_up = going_down = array
+    for far in range(1, ways // 2 + 1):
+        going_up = lax.ppermute(going_up, axis, [(d, (d + 1) % ways) for d in range(ways)])
+        full = lax.dynamic_update_slice_in_dim(full, going_up, (here - far) % ways * step, axis=dim)
+        if 2 * far < ways:
+            going_down = lax.ppermute(going_down, axis, [(d, (d - 1) % ways) for d in range(ways)])
+            full = lax.dynamic_update_slice_in_dim(
+                full, going_down, (here + far) % ways * step, axis=dim
+            )
+    return full
 
 
 def shifted(value, axis, by):
@@ -19,7 +37,7 @@
     blocks_here = idx.shape[1]
     w_blocks = w.reshape(KB, BLK, blocks_here, BLK)
     cols = idx[:, :, None] * BLK + jnp.arange(BLK, dtype=jnp.int32)[None, None, :]
-    full = lax.all_gather(y, "neuron", axis=1, tiled=True)
+    full = collect(y, "neuron", 1)
     taken = jnp.take(full, cols.reshape(-1), axis=1).reshape(rows, KB, blocks_here, BLK)
     acc = jnp.einsum("bkjr,krjc->bjc", taken, w_blocks, preferred_element_type=jnp.float32)
     acc = acc.reshape(rows, blocks_here * BLK)

time: 879 us -> 794 us (0.903)
  the two profiles are of different devices: /device:TPU:1 before, /device:TPU:256 now
where the time goes in v1:
time: 794 us; the launch traced here: 785 us
  local copies, waits for them, and re-layouts  401 us (51%)
  starting transfers between devices  278 us (35%)
  other arithmetic  53.1 us (7%)
  matrix products  27.3 us (3%)
  waiting for transfers between devices  22.5 us (3%)
    gather x4, local copies, waits for them, and re-layouts, run_layer(): jnp.take(full, cols.reshape(-1), axis=1).reshape(rows, KB, blocks_here, BLK)  251 us
    ppermute x28, starting transfers between devices, collect(): lax.ppermute(going_down, axis, [(d, (d - 1) % ways) for d in range(ways)])  201 us
    ppermute x32, starting transfers between devices, collect(): lax.ppermute(going_up, axis, [(d, (d + 1) % ways) for d in range(ways)])  74.8 us
    select_n x4, other arithmetic, run_layer(): jnp.take(full, cols.reshape(-1), axis=1).reshape(rows, KB, blocks_here, BLK)  43.7 us
    dynamic_update_slice x32, local copies, waits for them, and re-layouts, collect(): lax.dynamic_update_slice_in_dim(full, going_up, (here - far) % ways * ste...  34 us
    dynamic_update_slice x28, local copies, waits for them, and re-layouts, collect(): lax.dynamic_update_slice_in_dim(full, going_down, (here + far) % ways * s...  30 us
    dot_general x4, matrix products, run_layer(): jnp.einsum('bkjr,krjc->bjc', taken, w_blocks, preferred_element_type=jnp....  27.3 us
    another operation x4, local copies, waits for them, and re-layouts  24.3 us
  transfers between devices with their start and end apart: 61, of which 6 were waited for; matrix products, arithmetic and copies ran while one was open for 15% of the time, Pallas kernels for 0%

profile of v1, /device:TPU:256, one launch (start us, length us, event | category | flops | bytes accessed | tf_op | source)
XLA Modules:
  0.0 784.9 jit_solution(11501792205567751943)
XLA Ops:
  3.4 5.8 collective-permute-start.1
  17.0 6.1 broadcast.41.clone.2
  37.3 7.3 collective-permute-start.3
  49.6 7.2 collective-permute-start.5
  61.9 7.2 collective-permute-start.7
  74.2 7.2 collective-permute-start.9
  86.4 7.2 collective-permute-start.11
  98.7 7.2 collective-permute-start.13
  107.5 13.4 %collective-permute-start.14 = (bf16[8,4096]{1,0:T(8,128)(2,1)S(1)}, bf16[8,4096]{1,0:T(8,128)(2,1)S(1)}, u32[]{:S(2)}, u32[]{:S(2)}) collective-permute-start(bf16[8,4096]{1,0:T(8,128)(2,1)S(1)} %collective-permute-done.12), channel_id=1, source_target_pairs={{0,1},{1,2},{2,3},{3,4},{4,5},{5,6},{6,7},{7,8},{8,9},{9,10},{10,1... | collective-permute-start | bytes 196616 | tf_op jit(solution)/shard_map/ppermute | solution.py:19
  124.1 62.8 %gather_fusion = bf16[16384,8]{1,0:T(8,128)(2,1)} fusion(bf16[8,65536]{0,1:T(8,128)(2,1)} %constant_dynamic-update-slice_fusion.48, s32[16384]{0:T(1024)S(1)} %fusion.32), kind=kCustom, calls=%fused_computation.clone | custom fusion | bytes 589824 | tf_op jit(solution)/shard_map/jit(_take)/gather | solution.py:41
  186.9 10.9 %broadcast_select_fusion.2 = bf16[16384,8]{1,0:T(8,128)(2,1)S(1)} fusion(bf16[16384,8]{1,0:T(8,128)(2,1)} %gather_fusion, pred[16384]{0:T(1024)(128)(4,1)S(1)} %compare_and_fusion.1), kind=kLoop, calls=%fused_computation.6 | loop fusion | flops 131072 | bytes 540672 | tf_op jit(solution)/shard_map/jit(_take)/select_n | solution.py:41
  197.8 6.8 fusion.16
  206.7 6.1 broadcast.41.clone.1
  216.6 7.0 reshape_squeeze.9
  223.6 7.3 collective-permute-start.16
  235.9 7.3 collective-permute-start.18
  248.1 7.2 collective-permute-start.20
  260.4 7.2 collective-permute-start.22
  272.7 7.2 collective-permute-start.24
  285.0 7.2 collective-permute-start.26
  297.3 7.2 collective-permute-start.28
  317.2 62.8 %gather_fusion.1 = bf16[16384,8]{1,0:T(8,128)(2,1)} fusion(bf16[8,65536]{0,1:T(8,128)(2,1)} %constant_dynamic-update-slice_fusion.32, s32[16384]{0:T(1024)S(1)} %fusion.33), kind=kCustom, calls=%fused_computation.1.clone | custom fusion | bytes 589824 | tf_op jit(solution)/shard_map/jit(_take)/gather | solution.py:41
  380.0 10.9 %broadcast_select_fusion = bf16[16384,8]{1,0:T(8,128)(2,1)S(1)} fusion(bf16[16384,8]{1,0:T(8,128)(2,1)} %gather_fusion.1, pred[16384]{0:T(1024)(128)(4,1)S(1)} %compare_and_fusion), kind=kLoop, calls=%fused_computation.4 | loop fusion | flops 131072 | bytes 540672 | tf_op jit(solution)/shard_map/jit(_take)/select_n | solution.py:41
  390.9 6.8 fusion.22
  409.2 6.1 broadcast.41.clone
  418.8 7.2 collective-permute-start.32
  431.4 7.4 collective-permute-start.34
  443.8 7.2 collective-permute-start.36
  456.1 7.2 collective-permute-start.38
  468.4 7.2 collective-permute-start.40
  480.7 7.2 collective-permute-start.42
  493.0 7.2 collective-permute-start.44
  505.3 5.9 collective-permute-done.45
  512.7 62.8 %gather_fusion.2 = bf16[16384,8]{1,0:T(8,128)(2,1)} fusion(bf16[8,65536]{0,1:T(8,128)(2,1)} %constant_dynamic-update-slice_fusion.16, s32[16384]{0:T(1024)S(1)} %fusion.32), kind=kCustom, calls=%fused_computation.2.clone | custom fusion | bytes 589824 | tf_op jit(solution)/shard_map/jit(_take)/gather | solution.py:41
  575.5 10.9 %broadcast_select_fusion.3 = bf16[16384,8]{1,0:T(8,128)(2,1)S(1)} fusion(bf16[16384,8]{1,0:T(8,128)(2,1)} %gather_fusion.2, pred[16384]{0:T(1024)(128)(4,1)S(1)} %compare_and_fusion.1), kind=kLoop, calls=%fused_computation.7 | loop fusion | flops 131072 | bytes 540672 | tf_op jit(solution)/shard_map/jit(_take)/select_n | solution.py:41
  586.5 6.8 fusion.19
  595.3 6.1 broadcast.41
  605.2 7.2 collective-permute-start.47
  617.7 7.3 collective-permute-start.49
  630.0 7.2 collective-permute-start.51
  642.5 7.2 collective-permute-start.53
  654.8 7.2 collective-permute-start.55
  667.1 7.2 collective-permute-start.57
  679.4 7.2 collective-permute-start.59
  691.7 5.9 collective-permute-done.60
  699.1 62.8 %gather_fusion.3 = bf16[16384,8]{1,0:T(8,128)(2,1)} fusion(bf16[8,65536]{0,1:T(8,128)(2,1)} %constant_dynamic-update-slice_fusion, s32[16384]{0:T(1024)S(1)} %fusion.33), kind=kCustom, calls=%fused_computation.3.clone | custom fusion | bytes 589824 | tf_op jit(solution)/shard_map/jit(_take)/gather | solution.py:41
  761.9 10.9 %broadcast_select_fusion.1 = bf16[16384,8]{1,0:T(8,128)(2,1)S(1)} fusion(bf16[16384,8]{1,0:T(8,128)(2,1)} %gather_fusion.3, pred[16384]{0:T(1024)(128)(4,1)S(1)} %compare_and_fusion), kind=kLoop, calls=%fused_computation.5 | loop fusion | flops 131072 | bytes 540672 | tf_op jit(solution)/shard_map/jit(_take)/select_n | solution.py:41
  772.8 6.8 fusion.25
  (248 shorter events, 202.0 us)
Async XLA Ops:
  0.0 30.7 %collective-permute-start = (bf16[8,4096]{1,0:T(8,128)(2,1)}, bf16[8,4096]{1,0:T(8,128)(2,1)}, u32[]{:S(2)}, u32[]{:S(2)}) collective-permute-start(bf16[8,4096]{1,0:T(8,128)(2,1)} %bitcast.94), channel_id=1, source_target_pairs={{0,1},{1,2},{2,3},{3,4},{4,5},{5,6},{6,7},{7,8},{8,9},{9,10},{10,1... | collective-permute-start | bytes 196616 | tf_op jit(solution)/shard_map/ppermute | solution.py:19
  3.4 31.6 %collective-permute-start.1 = (bf16[8,4096]{1,0:T(8,128)(2,1)}, bf16[8,4096]{1,0:T(8,128)(2,1)}, u32[]{:S(2)}, u32[]{:S(2)}) collective-permute-start(bf16[8,4096]{1,0:T(8,128)(2,1)} %bitcast.95), channel_id=1, source_target_pairs={{0,15},{1,0},{2,1},{3,2},{4,3},{5,4},{6,5},{7,6},{8,7},{9,8},{10,9... | collective-permute-start | bytes 196616 | tf_op jit(solution)/shard_map/ppermute | solution.py:22
  33.0 11.6 %collective-permute-start.2 = (bf16[8,4096]{1,0:T(8,128)(2,1)}, bf16[8,4096]{1,0:T(8,128)(2,1)S(1)}, u32[]{:S(2)}, u32[]{:S(2)}) collective-permute-start(bf16[8,4096]{1,0:T(8,128)(2,1)} %collective-permute-done), channel_id=1, source_target_pairs={{0,1},{1,2},{2,3},{3,4},{4,5},{5,6},{6,7},{7,8},{8,9},{9,10},{10,1... | collective-permute-start | bytes 196616 | tf_op jit(solution)/shard_map/ppermute | solution.py:19
  37.3 10.7 %collective-permute-start.3 = (bf16[8,4096]{1,0:T(8,128)(2,1)}, bf16[8,4096]{1,0:T(8,128)(2,1)S(1)}, u32[]{:S(2)}, u32[]{:S(2)}) collective-permute-start(bf16[8,4096]{1,0:T(8,128)(2,1)} %collective-permute-done.1), channel_id=1, source_target_pairs={{0,15},{1,0},{2,1},{3,2},{4,3},{5,4},{6,5},{7,6},{8,7},{9,8},{10,9... | collective-permute-start | bytes 196616 | tf_op jit(solution)/shard_map/ppermute | solution.py:22
  46.2 10.7 %collective-permute-start.4 = (bf16[8,4096]{1,0:T(8,128)(2,1)S(1)}, bf16[8,4096]{1,0:T(8,128)(2,1)S(1)}, u32[]{:S(2)}, u32[]{:S(2)}) collective-permute-start(bf16[8,4096]{1,0:T(8,128)(2,1)S(1)} %collective-permute-done.2), channel_id=1, source_target_pairs={{0,1},{1,2},{2,3},{3,4},{4,5},{5,6},{6,7},{7,8},{8,9},{9,10},{10,1... | collective-permute-start | bytes 196616 | tf_op jit(solution)/shard_map/ppermute | solution.py:19
  49.6 10.7 %collective-permute-start.5 = (bf16[8,4096]{1,0:T(8,128)(2,1)S(1)}, bf16[8,4096]{1,0:T(8,128)(2,1)S(1)}, u32[]{:S(2)}, u32[]{:S(2)}) collective-permute-start(bf16[8,4096]{1,0:T(8,128)(2,1)S(1)} %collective-permute-done.3), channel_id=1, source_target_pairs={{0,15},{1,0},{2,1},{3,2},{4,3},{5,4},{6,5},{7,6},{8,7},{9,8},{10,9... | collective-permute-start | bytes 196616 | tf_op jit(solution)/shard_map/ppermute | solution.py:22
  58.4 10.7 %collective-permute-start.6 = (bf16[8,4096]{1,0:T(8,128)(2,1)S(1)}, bf16[8,4096]{1,0:T(8,128)(2,1)S(1)}, u32[]{:S(2)}, u32[]{:S(2)}) collective-permute-start(bf16[8,4096]{1,0:T(8,128)(2,1)S(1)} %collective-permute-done.4), channel_id=1, source_target_pairs={{0,1},{1,2},{2,3},{3,4},{4,5},{5,6},{6,7},{7,8},{8,9},{9,10},{10,1... | collective-permute-start | bytes 196616 | tf_op jit(solution)/shard_map/ppermute | solution.py:19
  61.9 10.7 %collective-permute-start.7 = (bf16[8,4096]{1,0:T(8,128)(2,1)S(1)}, bf16[8,4096]{1,0:T(8,128)(2,1)S(1)}, u32[]{:S(2)}, u32[]{:S(2)}) collective-permute-start(bf16[8,4096]{1,0:T(8,128)(2,1)S(1)} %collective-permute-done.5), channel_id=1, source_target_pairs={{0,15},{1,0},{2,1},{3,2},{4,3},{5,4},{6,5},{7,6},{8,7},{9,8},{10,9... | collective-permute-start | bytes 196616 | tf_op jit(solution)/shard_map/ppermute | solution.py:22
  74.2 10.7 %collective-permute-start.9 = (bf16[8,4096]{1,0:T(8,128)(2,1)S(1)}, bf16[8,4096]{1,0:T(8,128)(2,1)S(1)}, u32[]{:S(2)}, u32[]{:S(2)}) collective-permute-start(bf16[8,4096]{1,0:T(8,128)(2,1)S(1)} %collective-permute-done.7), channel_id=1, source_target_pairs={{0,15},{1,0},{2,1},{3,2},{4,3},{5,4},{6,5},{7,6},{8,7},{9,8},{10,9... | collective-permute-start | bytes 196616 | tf_op jit(solution)/shard_map/ppermute | solution.py:22
  83.0 10.7 %collective-permute-start.10 = (bf16[8,4096]{1,0:T(8,128)(2,1)S(1)}, bf16[8,4096]{1,0:T(8,128)(2,1)S(1)}, u32[]{:S(2)}, u32[]{:S(2)}) collective-permute-start(bf16[8,4096]{1,0:T(8,128)(2,1)S(1)} %collective-permute-done.8), channel_id=1, source_target_pairs={{0,1},{1,2},{2,3},{3,4},{4,5},{5,6},{6,7},{7,8},{8,9},{9,10},{10,1... | collective-permute-start | bytes 196616 | tf_op jit(solution)/shard_map/ppermute | solution.py:19
  86.4 10.7 %collective-permute-start.11 = (bf16[8,4096]{1,0:T(8,128)(2,1)S(1)}, bf16[8,4096]{1,0:T(8,128)(2,1)S(1)}, u32[]{:S(2)}, u32[]{:S(2)}) collective-permute-start(bf16[8,4096]{1,0:T(8,128)(2,1)S(1)} %collective-permute-done.9), channel_id=1, source_target_pairs={{0,15},{1,0},{2,1},{3,2},{4,3},{5,4},{6,5},{7,6},{8,7},{9,8},{10,9... | collective-permute-start | bytes 196616 | tf_op jit(solution)/shard_map/ppermute | solution.py:22
  95.3 10.7 %collective-permute-start.12 = (bf16[8,4096]{1,0:T(8,128)(2,1)S(1)}, bf16[8,4096]{1,0:T(8,128)(2,1)S(1)}, u32[]{:S(2)}, u32[]{:S(2)}) collective-permute-start(bf16[8,4096]{1,0:T(8,128)(2,1)S(1)} %collective-permute-done.10), channel_id=1, source_target_pairs={{0,1},{1,2},{2,3},{3,4},{4,5},{5,6},{6,7},{7,8},{8,9},{9,10},{10,1... | collective-permute-start | bytes 196616 | tf_op jit(solution)/shard_map/ppermute | solution.py:19
  98.7 22.2 %collective-permute-start.13 = (bf16[8,4096]{1,0:T(8,128)(2,1)S(1)}, bf16[8,4096]{1,0:T(8,128)(2,1)S(1)}, u32[]{:S(2)}, u32[]{:S(2)}) collective-permute-start(bf16[8,4096]{1,0:T(8,128)(2,1)S(1)} %collective-permute-done.11), channel_id=1, source_target_pairs={{0,15},{1,0},{2,1},{3,2},{4,3},{5,4},{6,5},{7,6},{8,7},{9,8},{10,9... | collective-permute-start | bytes 196616 | tf_op jit(solution)/shard_map/ppermute | solution.py:22
  107.5 15.0 %collective-permute-start.14 = (bf16[8,4096]{1,0:T(8,128)(2,1)S(1)}, bf16[8,4096]{1,0:T(8,128)(2,1)S(1)}, u32[]{:S(2)}, u32[]{:S(2)}) collective-permute-start(bf16[8,4096]{1,0:T(8,128)(2,1)S(1)} %collective-permute-done.12), channel_id=1, source_target_pairs={{0,1},{1,2},{2,3},{3,4},{4,5},{5,6},{6,7},{7,8},{8,9},{9,10},{10,1... | collective-permute-start | bytes 196616 | tf_op jit(solution)/shard_map/ppermute | solution.py:19
  214.7 16.2 %collective-permute-start.15 = (bf16[8,4096]{1,0:T(8,128)(2,1)S(1)}, bf16[8,4096]{1,0:T(8,128)(2,1)S(1)}, u32[]{:S(2)}, u32[]{:S(2)}) collective-permute-start(bf16[8,4096]{1,0:T(8,128)(2,1)S(1)} %copy.56), channel_id=1, source_target_pairs={{0,1},{1,2},{2,3},{3,4},{4,5},{5,6},{6,7},{7,8},{8,9},{9,10},{10,1... | collective-permute-start | bytes 196616 | tf_op jit(solution)/shard_map/ppermute | solution.py:19
  223.6 10.7 %collective-permute-start.16 = (bf16[8,4096]{1,0:T(8,128)(2,1)S(1)}, bf16[8,4096]{1,0:T(8,128)(2,1)S(1)}, u32[]{:S(2)}, u32[]{:S(2)}) collective-permute-start(bf16[8,4096]{1,0:T(8,128)(2,1)S(1)} %copy.56), channel_id=1, source_target_pairs={{0,15},{1,0},{2,1},{3,2},{4,3},{5,4},{6,5},{7,6},{8,7},{9,8},{10,9... | collective-permute-start | bytes 196616 | tf_op jit(solution)/shard_map/ppermute | solution.py:22
  232.4 10.8 %collective-permute-start.17 = (bf16[8,4096]{1,0:T(8,128)(2,1)S(1)}, bf16[8,4096]{1,0:T(8,128)(2,1)S(1)}, u32[]{:S(2)}, u32[]{:S(2)}) collective-permute-start(bf16[8,4096]{1,0:T(8,128)(2,1)S(1)} %collective-permute-done.15), channel_id=1, source_target_pairs={{0,1},{1,2},{2,3},{3,4},{4,5},{5,6},{6,7},{7,8},{8,9},{9,10},{10,1... | collective-permute-start | bytes 196616 | tf_op jit(solution)/shard_map/ppermute | solution.py:19
  235.9 10.7 %collective-permute-start.18 = (bf16[8,4096]{1,0:T(8,128)(2,1)S(1)}, bf16[8,4096]{1,0:T(8,128)(2,1)S(1)}, u32[]{:S(2)}, u32[]{:S(2)}) collective-permute-start(bf16[8,4096]{1,0:T(8,128)(2,1)S(1)} %collective-permute-done.16), channel_id=1, source_target_pairs={{0,15},{1,0},{2,1},{3,2},{4,3},{5,4},{6,5},{7,6},{8,7},{9,8},{10,9... | collective-permute-start | bytes 196616 | tf_op jit(solution)/shard_map/ppermute | solution.py:22
  244.7 10.7 %collective-permute-start.19 = (bf16[8,4096]{1,0:T(8,128)(2,1)S(1)}, bf16[8,4096]{1,0:T(8,128)(2,1)S(1)}, u32[]{:S(2)}, u32[]{:S(2)}) collective-permute-start(bf16[8,4096]{1,0:T(8,128)(2,1)S(1)} %collective-permute-done.17), channel_id=1, source_target_pairs={{0,1},{1,2},{2,3},{3,4},{4,5},{5,6},{6,7},{7,8},{8,9},{9,10},{10,1... | collective-permute-start | bytes 196616 | tf_op jit(solution)/shard_map/ppermute | solution.py:19
  248.1 10.7 %collective-permute-start.20 = (bf16[8,4096]{1,0:T(8,128)(2,1)S(1)}, bf16[8,4096]{1,0:T(8,128)(2,1)S(1)}, u32[]{:S(2)}, u32[]{:S(2)}) collective-permute-start(bf16[8,4096]{1,0:T(8,128)(2,1)S(1)} %collective-permute-done.18), channel_id=1, source_target_pairs={{0,15},{1,0},{2,1},{3,2},{4,3},{5,4},{6,5},{7,6},{8,7},{9,8},{10,9... | collective-permute-start | bytes 196616 | tf_op jit(solution)/shard_map/ppermute | solution.py:22
  256.9 10.7 %collective-permute-start.21 = (bf16[8,4096]{1,0:T(8,128)(2,1)S(1)}, bf16[8,4096]{1,0:T(8,128)(2,1)S(1)}, u32[]{:S(2)}, u32[]{:S(2)}) collective-permute-start(bf16[8,4096]{1,0:T(8,128)(2,1)S(1)} %collective-permute-done.19), channel_id=1, source_target_pairs={{0,1},{1,2},{2,3},{3,4},{4,5},{5,6},{6,7},{7,8},{8,9},{9,10},{10,1... | collective-permute-start | bytes 196616 | tf_op jit(solution)/shard_map/ppermute | solution.py:19
  260.4 10.7 %collective-permute-start.22 = (bf16[8,4096]{1,0:T(8,128)(2,1)S(1)}, bf16[8,4096]{1,0:T(8,128)(2,1)S(1)}, u32[]{:S(2)}, u32[]{:S(2)}) collective-permute-start(bf16[8,4096]{1,0:T(8,128)(2,1)S(1)} %collective-permute-done.20), channel_id=1, source_target_pairs={{0,15},{1,0},{2,1},{3,2},{4,3},{5,4},{6,5},{7,6},{8,7},{9,8},{10,9... | collective-permute-start | bytes 196616 | tf_op jit(solution)/shard_map/ppermute | solution.py:22
  272.7 10.7 %collective-permute-start.24 = (bf16[8,4096]{1,0:T(8,128)(2,1)S(1)}, bf16[8,4096]{1,0:T(8,128)(2,1)S(1)}, u32[]{:S(2)}, u32[]{:S(2)}) collective-permute-start(bf16[8,4096]{1,0:T(8,128)(2,1)S(1)} %collective-permute-done.22), channel_id=1, source_target_pairs={{0,15},{1,0},{2,1},{3,2},{4,3},{5,4},{6,5},{7,6},{8,7},{9,8},{10,9... | collective-permute-start | bytes 196616 | tf_op jit(solution)/shard_map/ppermute | solution.py:22
  281.5 10.7 %collective-permute-start.25 = (bf16[8,4096]{1,0:T(8,128)(2,1)S(1)}, bf16[8,4096]{1,0:T(8,128)(2,1)S(1)}, u32[]{:S(2)}, u32[]{:S(2)}) collective-permute-start(bf16[8,4096]{1,0:T(8,128)(2,1)S(1)} %collective-permute-done.23), channel_id=1, source_target_pairs={{0,1},{1,2},{2,3},{3,4},{4,5},{5,6},{6,7},{7,8},{8,9},{9,10},{10,1... | collective-permute-start | bytes 196616 | tf_op jit(solution)/shard_map/ppermute | solution.py:19
  285.0 10.7 %collective-permute-start.26 = (bf16[8,4096]{1,0:T(8,128)(2,1)S(1)}, bf16[8,4096]{1,0:T(8,128)(2,1)S(1)}, u32[]{:S(2)}, u32[]{:S(2)}) collective-permute-start(bf16[8,4096]{1,0:T(8,128)(2,1)S(1)} %collective-permute-done.24), channel_id=1, source_target_pairs={{0,15},{1,0},{2,1},{3,2},{4,3},{5,4},{6,5},{7,6},{8,7},{9,8},{10,9... | collective-permute-start | bytes 196616 | tf_op jit(solution)/shard_map/ppermute | solution.py:22
  293.8 10.7 %collective-permute-start.27 = (bf16[8,4096]{1,0:T(8,128)(2,1)S(1)}, bf16[8,4096]{1,0:T(8,128)(2,1)S(1)}, u32[]{:S(2)}, u32[]{:S(2)}) collective-permute-start(bf16[8,4096]{1,0:T(8,128)(2,1)S(1)} %collective-permute-done.25), channel_id=1, source_target_pairs={{0,1},{1,2},{2,3},{3,4},{4,5},{5,6},{6,7},{7,8},{8,9},{9,10},{10,1... | collective-permute-start | bytes 196616 | tf_op jit(solution)/shard_map/ppermute | solution.py:19
  297.3 11.2 %collective-permute-start.28 = (bf16[8,4096]{1,0:T(8,128)(2,1)S(1)}, bf16[8,4096]{1,0:T(8,128)(2,1)S(1)}, u32[]{:S(2)}, u32[]{:S(2)}) collective-permute-start(bf16[8,4096]{1,0:T(8,128)(2,1)S(1)} %collective-permute-done.26), channel_id=1, source_target_pairs={{0,15},{1,0},{2,1},{3,2},{4,3},{5,4},{6,5},{7,6},{8,7},{9,8},{10,9... | collective-permute-start | bytes 196616 | tf_op jit(solution)/shard_map/ppermute | solution.py:22
  418.8 11.0 %collective-permute-start.32 = (bf16[8,4096]{1,0:T(8,128)(2,1)S(1)}, bf16[8,4096]{1,0:T(8,128)(2,1)S(1)}, u32[]{:S(2)}, u32[]{:S(2)}) collective-permute-start(bf16[8,4096]{1,0:T(8,128)(2,1)S(1)} %copy.79), channel_id=1, source_target_pairs={{0,15},{1,0},{2,1},{3,2},{4,3},{5,4},{6,5},{7,6},{8,7},{9,8},{10,9... | collective-permute-start | bytes 196616 | tf_op jit(solution)/shard_map/ppermute | solution.py:22
  427.9 10.9 %collective-permute-start.33 = (bf16[8,4096]{1,0:T(8,128)(2,1)S(1)}, bf16[8,4096]{1,0:T(8,128)(2,1)S(1)}, u32[]{:S(2)}, u32[]{:S(2)}) collective-permute-start(bf16[8,4096]{1,0:T(8,128)(2,1)S(1)} %collective-permute-done.31), channel_id=1, source_target_pairs={{0,1},{1,2},{2,3},{3,4},{4,5},{5,6},{6,7},{7,8},{8,9},{9,10},{10,1... | collective-permute-start | bytes 196616 | tf_op jit(solution)/shard_map/ppermute | solution.py:19
  431.4 10.9 %collective-permute-start.34 = (bf16[8,4096]{1,0:T(8,128)(2,1)S(1)}, bf16[8,4096]{1,0:T(8,128)(2,1)S(1)}, u32[]{:S(2)}, u32[]{:S(2)}) collective-permute-start(bf16[8,4096]{1,0:T(8,128)(2,1)S(1)} %collective-permute-done.32), channel_id=1, source_target_pairs={{0,15},{1,0},{2,1},{3,2},{4,3},{5,4},{6,5},{7,6},{8,7},{9,8},{10,9... | collective-permute-start | bytes 196616 | tf_op jit(solution)/shard_map/ppermute | solution.py:22
  440.4 10.7 %collective-permute-start.35 = (bf16[8,4096]{1,0:T(8,128)(2,1)S(1)}, bf16[8,4096]{1,0:T(8,128)(2,1)S(1)}, u32[]{:S(2)}, u32[]{:S(2)}) collective-permute-start(bf16[8,4096]{1,0:T(8,128)(2,1)S(1)} %collective-permute-done.33), channel_id=1, source_target_pairs={{0,1},{1,2},{2,3},{3,4},{4,5},{5,6},{6,7},{7,8},{8,9},{9,10},{10,1... | collective-permute-start | bytes 196616 | tf_op jit(solution)/shard_map/ppermute | solution.py:19
  443.8 10.7 %collective-permute-start.36 = (bf16[8,4096]{1,0:T(8,128)(2,1)S(1)}, bf16[8,4096]{1,0:T(8,128)(2,1)S(1)}, u32[]{:S(2)}, u32[]{:S(2)}) collective-permute-start(bf16[8,4096]{1,0:T(8,128)(2,1)S(1)} %collective-permute-done.34), channel_id=1, source_target_pairs={{0,15},{1,0},{2,1},{3,2},{4,3},{5,4},{6,5},{7,6},{8,7},{9,8},{10,9... | collective-permute-start | bytes 196616 | tf_op jit(solution)/shard_map/ppermute | solution.py:22
  456.1 10.7 %collective-permute-start.38 = (bf16[8,4096]{1,0:T(8,128)(2,1)S(1)}, bf16[8,4096]{1,0:T(8,128)(2,1)S(1)}, u32[]{:S(2)}, u32[]{:S(2)}) collective-permute-start(bf16[8,4096]{1,0:T(8,128)(2,1)S(1)} %collective-permute-done.36), channel_id=1, source_target_pairs={{0,15},{1,0},{2,1},{3,2},{4,3},{5,4},{6,5},{7,6},{8,7},{9,8},{10,9... | collective-permute-start | bytes 196616 | tf_op jit(solution)/shard_map/ppermute | solution.py:22
  468.4 10.7 %collective-permute-start.40 = (bf16[8,4096]{1,0:T(8,128)(2,1)S(1)}, bf16[8,4096]{1,0:T(8,128)(2,1)S(1)}, u32[]{:S(2)}, u32[]{:S(2)}) collective-permute-start(bf16[8,4096]{1,0:T(8,128)(2,1)S(1)} %collective-permute-done.38), channel_id=1, source_target_pairs={{0,15},{1,0},{2,1},{3,2},{4,3},{5,4},{6,5},{7,6},{8,7},{9,8},{10,9... | collective-permute-start | bytes 196616 | tf_op jit(solution)/shard_map/ppermute | solution.py:22
  477.2 10.7 %collective-permute-start.41 = (bf16[8,4096]{1,0:T(8,128)(2,1)S(1)}, bf16[8,4096]{1,0:T(8,128)(2,1)S(1)}, u32[]{:S(2)}, u32[]{:S(2)}) collective-permute-start(bf16[8,4096]{1,0:T(8,128)(2,1)S(1)} %collective-permute-done.39), channel_id=1, source_target_pairs={{0,1},{1,2},{2,3},{3,4},{4,5},{5,6},{6,7},{7,8},{8,9},{9,10},{10,1... | collective-permute-start | bytes 196616 | tf_op jit(solution)/shard_map/ppermute | solution.py:19
  480.7 10.7 %collective-permute-start.42 = (bf16[8,4096]{1,0:T(8,128)(2,1)S(1)}, bf16[8,4096]{1,0:T(8,128)(2,1)S(1)}, u32[]{:S(2)}, u32[]{:S(2)}) collective-permute-start(bf16[8,4096]{1,0:T(8,128)(2,1)S(1)} %collective-permute-done.40), channel_id=1, source_target_pairs={{0,15},{1,0},{2,1},{3,2},{4,3},{5,4},{6,5},{7,6},{8,7},{9,8},{10,9... | collective-permute-start | bytes 196616 | tf_op jit(solution)/shard_map/ppermute | solution.py:22
  489.5 10.7 %collective-permute-start.43 = (bf16[8,4096]{1,0:T(8,128)(2,1)S(1)}, bf16[8,4096]{1,0:T(8,128)(2,1)S(1)}, u32[]{:S(2)}, u32[]{:S(2)}) collective-permute-start(bf16[8,4096]{1,0:T(8,128)(2,1)S(1)} %collective-permute-done.41), channel_id=1, source_target_pairs={{0,1},{1,2},{2,3},{3,4},{4,5},{5,6},{6,7},{7,8},{8,9},{9,10},{10,1... | collective-permute-start | bytes 196616 | tf_op jit(solution)/shard_map/ppermute | solution.py:19
  605.2 11.0 %collective-permute-start.47 = (bf16[8,4096]{1,0:T(8,128)(2,1)S(1)}, bf16[8,4096]{1,0:T(8,128)(2,1)S(1)}, u32[]{:S(2)}, u32[]{:S(2)}) collective-permute-start(bf16[8,4096]{1,0:T(8,128)(2,1)S(1)} %copy.100), channel_id=1, source_target_pairs={{0,15},{1,0},{2,1},{3,2},{4,3},{5,4},{6,5},{7,6},{8,7},{9,8},{10,9... | collective-permute-start | bytes 196616 | tf_op jit(solution)/shard_map/ppermute | solution.py:22
  614.3 10.8 %collective-permute-start.48 = (bf16[8,4096]{1,0:T(8,128)(2,1)S(1)}, bf16[8,4096]{1,0:T(8,128)(2,1)S(1)}, u32[]{:S(2)}, u32[]{:S(2)}) collective-permute-start(bf16[8,4096]{1,0:T(8,128)(2,1)S(1)} %collective-permute-done.46), channel_id=1, source_target_pairs={{0,1},{1,2},{2,3},{3,4},{4,5},{5,6},{6,7},{7,8},{8,9},{9,10},{10,1... | collective-permute-start | bytes 196616 | tf_op jit(solution)/shard_map/ppermute | solution.py:19
  617.7 10.7 %collective-permute-start.49 = (bf16[8,4096]{1,0:T(8,128)(2,1)S(1)}, bf16[8,4096]{1,0:T(8,128)(2,1)S(1)}, u32[]{:S(2)}, u32[]{:S(2)}) collective-permute-start(bf16[8,4096]{1,0:T(8,128)(2,1)S(1)} %collective-permute-done.47), channel_id=1, source_target_pairs={{0,15},{1,0},{2,1},{3,2},{4,3},{5,4},{6,5},{7,6},{8,7},{9,8},{10,9... | collective-permute-start | bytes 196616 | tf_op jit(solution)/shard_map/ppermute | solution.py:22
  626.6 10.7 %collective-permute-start.50 = (bf16[8,4096]{1,0:T(8,128)(2,1)S(1)}, bf16[8,4096]{1,0:T(8,128)(2,1)S(1)}, u32[]{:S(2)}, u32[]{:S(2)}) collective-permute-start(bf16[8,4096]{1,0:T(8,128)(2,1)S(1)} %collective-permute-done.48), channel_id=1, source_target_pairs={{0,1},{1,2},{2,3},{3,4},{4,5},{5,6},{6,7},{7,8},{8,9},{9,10},{10,1... | collective-permute-start | bytes 196616 | tf_op jit(solution)/shard_map/ppermute | solution.py:19
  630.0 10.9 %collective-permute-start.51 = (bf16[8,4096]{1,0:T(8,128)(2,1)S(1)}, bf16[8,4096]{1,0:T(8,128)(2,1)S(1)}, u32[]{:S(2)}, u32[]{:S(2)}) collective-permute-start(bf16[8,4096]{1,0:T(8,128)(2,1)S(1)} %collective-permute-done.49), channel_id=1, source_target_pairs={{0,15},{1,0},{2,1},{3,2},{4,3},{5,4},{6,5},{7,6},{8,7},{9,8},{10,9... | collective-permute-start | bytes 196616 | tf_op jit(solution)/shard_map/ppermute | solution.py:22
  638.8 10.9 %collective-permute-start.52 = (bf16[8,4096]{1,0:T(8,128)(2,1)S(1)}, bf16[8,4096]{1,0:T(8,128)(2,1)S(1)}, u32[]{:S(2)}, u32[]{:S(2)}) collective-permute-start(bf16[8,4096]{1,0:T(8,128)(2,1)S(1)} %collective-permute-done.50), channel_id=1, source_target_pairs={{0,1},{1,2},{2,3},{3,4},{4,5},{5,6},{6,7},{7,8},{8,9},{9,10},{10,1... | collective-permute-start | bytes 196616 | tf_op jit(solution)/shard_map/ppermute | solution.py:19
  642.5 10.7 %collective-permute-start.53 = (bf16[8,4096]{1,0:T(8,128)(2,1)S(1)}, bf16[8,4096]{1,0:T(8,128)(2,1)S(1)}, u32[]{:S(2)}, u32[]{:S(2)}) collective-permute-start(bf16[8,4096]{1,0:T(8,128)(2,1)S(1)} %collective-permute-done.51), channel_id=1, source_target_pairs={{0,15},{1,0},{2,1},{3,2},{4,3},{5,4},{6,5},{7,6},{8,7},{9,8},{10,9... | collective-permute-start | bytes 196616 | tf_op jit(solution)/shard_map/ppermute | solution.py:22
  654.8 10.7 %collective-permute-start.55 = (bf16[8,4096]{1,0:T(8,128)(2,1)S(1)}, bf16[8,4096]{1,0:T(8,128)(2,1)S(1)}, u32[]{:S(2)}, u32[]{:S(2)}) collective-permute-start(bf16[8,4096]{1,0:T(8,128)(2,1)S(1)} %collective-permute-done.53), channel_id=1, source_target_pairs={{0,15},{1,0},{2,1},{3,2},{4,3},{5,4},{6,5},{7,6},{8,7},{9,8},{10,9... | collective-permute-start | bytes 196616 | tf_op jit(solution)/shard_map/ppermute | solution.py:22
  663.6 10.7 %collective-permute-start.56 = (bf16[8,4096]{1,0:T(8,128)(2,1)S(1)}, bf16[8,4096]{1,0:T(8,128)(2,1)S(1)}, u32[]{:S(2)}, u32[]{:S(2)}) collective-permute-start(bf16[8,4096]{1,0:T(8,128)(2,1)S(1)} %collective-permute-done.54), channel_id=1, source_target_pairs={{0,1},{1,2},{2,3},{3,4},{4,5},{5,6},{6,7},{7,8},{8,9},{9,10},{10,1... | collective-permute-start | bytes 196616 | tf_op jit(solution)/shard_map/ppermute | solution.py:19
  667.1 10.7 %collective-permute-start.57 = (bf16[8,4096]{1,0:T(8,128)(2,1)S(1)}, bf16[8,4096]{1,0:T(8,128)(2,1)S(1)}, u32[]{:S(2)}, u32[]{:S(2)}) collective-permute-start(bf16[8,4096]{1,0:T(8,128)(2,1)S(1)} %collective-permute-done.55), channel_id=1, source_target_pairs={{0,15},{1,0},{2,1},{3,2},{4,3},{5,4},{6,5},{7,6},{8,7},{9,8},{10,9... | collective-permute-start | bytes 196616 | tf_op jit(solution)/shard_map/ppermute | solution.py:22
  675.9 10.7 %collective-permute-start.58 = (bf16[8,4096]{1,0:T(8,128)(2,1)S(1)}, bf16[8,4096]{1,0:T(8,128)(2,1)S(1)}, u32[]{:S(2)}, u32[]{:S(2)}) collective-permute-start(bf16[8,4096]{1,0:T(8,128)(2,1)S(1)} %collective-permute-done.56), channel_id=1, source_target_pairs={{0,1},{1,2},{2,3},{3,4},{4,5},{5,6},{6,7},{7,8},{8,9},{9,10},{10,1... | collective-permute-start | bytes 196616 | tf_op jit(solution)/shard_map/ppermute | solution.py:19
  (17 other events, 265.0 us)
